TPU v7x, 32 devices: a whole 2x2x4 slice. The times are simulated.
32 devices in a mesh: gx: 8 (over z, y), gy: 4 (over x, core).
Axes of the slice: x: 2, y: 2, z: 4, core: 2. Of those that a mesh axis runs over, the one named last changes fastest.
Arguments:
- saved_fractions: float32 [8, 16, 128, 512], P(None, None, 'gx', 'gy'), may hold values from 0 to 1
- adjoint_seed: bfloat16 [8, 16, 128, 512], P(None, None, 'gx', 'gy'), may hold values from -6 to 6
- slot_ids: int32 [8, 128, 512], P(None, 'gx', 'gy'), may hold values from 0 to 255, as said below
- active_counts: int32 [128, 512], P('gx', 'gy'), may hold values from 1 to 8
- mobility: float32 [256], replicated, may hold values from 0.5 to 2
- owner_pos: int32 [256], replicated, may hold values from 0 to 255, each once
- saved_instant: int32 [1], replicated, may hold values from 0 to 999
Outputs:
- phase_adjoint: float32 [8, 16, 128, 512], P(None, None, 'gx', 'gy')
- grain_gradient: float32 [256], P(('gx', 'gy'))
Inputs may be any that keep to these rules, and one draw needn't show every extreme that they name: `slot_ids`: the 8 ids of a column are distinct, and every grain is the first slot's grain of some column.
All inputs are finite; a program needn't handle non-finite values.
Results may differ from a plain program's by a relative error of at most 0.0005.
Values sent between devices are 32-bit elements; how exact they have to be, the bound alone decides.
A program may use at most 192 MiB of HBM per device.

v0:
```python
import jax
import jax.numpy as jnp
from jax import lax
from jax.sharding import PartitionSpec as P

EXPLICIT_UPDATES = 4


DT = 0.05
C_WELL = 1.0
C_PAIR = 0.25
OFFSETS = ((0, 1), (2, 1), (1, 0), (1, 2))


def passed_along(x, axis, by):
    count = lax.axis_size(axis)
    return lax.ppermute(x, axis, [(i, (i + by) % count) for i in range(count)])


def padded(block, sides, width):
    for axis, dim in sides:
        count = lax.axis_size(axis)
        forward = [(i, i + 1) for i in range(count - 1)]
        forward.append((count - 1, 0))
        backward = [(target, source) for source, target in forward]
        low = lax.ppermute(
            lax.slice_in_dim(block, block.shape[dim] - width, None, axis=dim), axis, forward
        )
        high = lax.ppermute(lax.slice_in_dim(block, 0, width, axis=dim), axis, backward)
        block = jnp.concatenate([low, block, high], axis=dim)
    return block


def thermal_map(saved_instant, update_interval):
    return 0.75 + 0.5 * jnp.cos(0.3 * (saved_instant[0].astype(jnp.float32) + update_interval))


def neighbor_matches(live_pad):
    width_a = live_pad.shape[1] - 2
    width_b = live_pad.shape[2] - 2
    centre = live_pad[:, 1 : width_a + 1, 1 : width_b + 1]
    result = []
    for dx, dy in OFFSETS:
        beside = live_pad[:, dx : dx + width_a, dy : dy + width_b]
        result.append(centre[:, None] == beside[None, :])
    return result


def update_fractions(phase_pad, crystal_equality, present_crystals, moving_crystals, factor):
    width_a = present_crystals.shape[1]
    width_b = present_crystals.shape[2]
    centre = phase_pad[:, :, 1 : width_a + 1, 1 : width_b + 1]
    total = jnp.zeros_like(centre)
    for index, (dx, dy) in enumerate(OFFSETS):
        beside = phase_pad[:, :, dx : dx + width_a, dy : dy + width_b]
        for slot in range(beside.shape[0]):
            total = total + jnp.where(
                crystal_equality[index][:, slot][:, None], beside[slot][None], 0.0
            )
    above = jnp.concatenate([centre[:, 1:], centre[:, -1:]], axis=1)
    below = jnp.concatenate([centre[:, :1], centre[:, :-1]], axis=1)
    laplace = total + above + below - 6.0 * centre
    occupied = jnp.sum(centre * present_crystals[:, None], axis=0)
    drive = (
        laplace
        + C_WELL * centre * (1.0 - centre) * (centre - 0.5)
        - C_PAIR * centre * (occupied[None] - centre)
    )
    return centre + DT * factor * (present_crystals * moving_crystals)[:, None] * drive


def slot_onehot(ids_plane, grains):
    codes = jnp.arange(grains, dtype=jnp.int32)
    return (ids_plane.reshape(-1)[:, None] == codes[None, :]).astype(jnp.float32)


def table_lookup(ids, table):
    grains = table.shape[0]
    planes = []
    for slot in range(ids.shape[0]):
        onehot = slot_onehot(ids[slot], grains)
        value = jnp.dot(onehot, table, precision=lax.Precision.HIGHEST)
        planes.append(value.reshape(ids.shape[1:]))
    return jnp.stack(planes)


def grain_totals(ids, values, grains):
    total = jnp.zeros((grains,), jnp.float32)
    for slot in range(ids.shape[0]):
        onehot = slot_onehot(ids[slot], grains)
        total = total + jnp.dot(values[slot].reshape(-1), onehot, precision=lax.Precision.HIGHEST)
    return total


def return_rims(cycle_cot):
    rows = cycle_cot.shape[2] - 2
    cols = cycle_cot.shape[3] - 2
    inner = cycle_cot[:, :, 1 : rows + 1, 1 : cols + 1]
    for by in (1, -1):
        face = cycle_cot[:, :, rows + 1 if by == 1 else 0, 1 : cols + 1]
        arrived = passed_along(face, "gx", by)
        inner = inner.at[:, :, 0 if by == 1 else rows - 1, :].add(arrived)
    for by in (1, -1):
        face = cycle_cot[:, :, 1 : rows + 1, cols + 1 if by == 1 else 0]
        arrived = passed_along(face, "gy", by)
        inner = inner.at[:, :, :, 0 if by == 1 else cols - 1].add(arrived)
    return inner


def shards(
    saved_fractions, adjoint_seed, slot_ids, active_counts, mobility, owner_pos, saved_instant
):
    slots, rows, cols = slot_ids.shape
    grains = mobility.shape[0]
    slot_index = jnp.arange(slots, dtype=jnp.int32)[:, None, None]
    live = jnp.where(slot_index < active_counts[None], slot_ids, -1)
    present_crystals = (live >= 0).astype(jnp.float32)
    mob_centre = table_lookup(slot_ids, mobility)
    order_parameter = saved_fractions * present_crystals[:, None]
    mobility_factors = [
        thermal_map(saved_instant, update_interval) for update_interval in range(EXPLICIT_UPDATES)
    ]
    states = []
    live_pad = padded(live, (("gx", 1), ("gy", 2)), 1)
    crystal_equality = neighbor_matches(live_pad)
    for update_interval in range(EXPLICIT_UPDATES):
        sweep_interval = padded(order_parameter, (("gx", 2), ("gy", 3)), 1)
        states.append(sweep_interval)
        if update_interval + 1 < EXPLICIT_UPDATES:
            order_parameter = update_fractions(
                sweep_interval,
                crystal_equality,
                present_crystals,
                mob_centre,
                mobility_factors[update_interval],
            )
    adjoint = adjoint_seed.astype(jnp.float32)
    mob_grad = jnp.zeros((slots, rows, cols), jnp.float32)
    for update_interval in reversed(range(EXPLICIT_UPDATES)):
        factor = mobility_factors[update_interval]

        def local_step(sweep_interval, moving_crystals):
            return update_fractions(
                sweep_interval, crystal_equality, present_crystals, moving_crystals, factor
            )

        _, pull = jax.vjp(local_step, states[update_interval], mob_centre)
        cycle_cot, mob_cot = pull(adjoint)
        mob_grad = mob_grad + mob_cot
        adjoint = return_rims(cycle_cot)
    phase_adjoint = adjoint * present_crystals[:, None]
    by_grain = grain_totals(slot_ids, mob_grad, grains)
    codes = jnp.arange(grains, dtype=jnp.int32)
    placement = (owner_pos[:, None] == codes[None, :]).astype(jnp.float32)
    partial_value = jnp.dot(by_grain, placement, precision=lax.Precision.HIGHEST)
    owned = lax.psum_scatter(partial_value, ("gx", "gy"), scatter_dimension=0, tiled=True)
    return (phase_adjoint, owned)


def solution(mesh):
    placed = (
        P(None, None, "gx", "gy"),
        P(None, None, "gx", "gy"),
        P(None, "gx", "gy"),
        P("gx", "gy"),
        P(),
        P(),
        P(),
    )
    return jax.shard_map(
        shards,
        mesh=mesh,
        in_specs=placed,
        out_specs=(P(None, None, "gx", "gy"), P(("gx", "gy"))),
        check_vma=False,
    )
```

profile of v0, /device:TPU:0, one launch (start us, length us, event | category | flops | bytes accessed | tf_op | source)
XLA Modules:
  0.0 462.6 jit_solution(15654063381200478577)
XLA Ops:
  18.8 4.7 %collective-permute-start.1 = (s32[8,1,128]{2,0,1:T(8,128)S(1)}, s32[8,1,128]{2,0,1:T(8,128)S(1)}, u32[]{:S(2)}, u32[]{:S(2)}) collective-permute-start(s32[8,1,128]{2,0,1:T(8,128)S(1)} %get-tuple-element.598), channel_id=1, source_target_pairs={{4,0},{8,4},{12,8},{16,12},{20,16},{24,20},{28,24},{0,28},{5,1},{9... | collective-permute-start | bytes 12296 | tf_op jit(solution)/shard_map/ppermute | solution.py:29
  32.0 4.5 fusion.110
  59.5 10.1 %multiply_reduce_fusion.5 = (f32[16,16,128]{2,0,1:T(8,128)}, f32[8,16,16,128]{3,1,0,2:T(8,128)S(1)}, f32[8,16,16,128]{3,1,0,2:T(8,128)}) fusion(f32[8,16,128]{2,0,1:T(8,128)S(1)} %convert_element_type.9, f32[8,16,16,128]{3,1,0,2:T(8,128)S(1)} %get-tuple-element.360, f32[8,16,128]{2,0,1:T(8,128)S(1)} %copy-done.180, f32[16,16,128]{2,0,1:T(8,128)S(1)} %copy-done.112, ...), kind=kLoop, calls=%fused_computation.302 | loop fusion | flops 21463040 | bytes 10354688 | tf_op jit(solution)/shard_map/reduce_sum | solution.py:63
  71.2 4.7 %collective-permute-start.9 = (f32[8,16,1,128]{3,1,0,2:T(8,128)S(1)}, f32[8,16,1,128]{3,1,0,2:T(8,128)S(1)}, u32[]{:S(2)}, u32[]{:S(2)}) collective-permute-start(f32[8,16,1,128]{3,1,0,2:T(8,128)S(1)} %get-tuple-element.540), channel_id=1, source_target_pairs={{4,0},{8,4},{12,8},{16,12},{20,16},{24,20},{28,24},{0,28},{5,1},{9... | collective-permute-start | bytes 196616 | tf_op jit(solution)/shard_map/ppermute | solution.py:29
  96.9 10.1 %multiply_reduce_fusion.4 = (f32[16,16,128]{2,0,1:T(8,128)}, f32[8,16,16,128]{3,1,0,2:T(8,128)S(1)}, f32[8,16,16,128]{3,1,0,2:T(8,128)}) fusion(f32[8,16,128]{2,0,1:T(8,128)S(1)} %convert_element_type.9, f32[8,16,16,128]{3,1,0,2:T(8,128)S(1)} %get-tuple-element.357, f32[8,16,128]{2,0,1:T(8,128)S(1)} %copy-done.181, f32[16,16,128]{2,0,1:T(8,128)S(1)} %copy-done.108, ...), kind=kLoop, calls=%fused_computation.300 | loop fusion | flops 21463040 | bytes 10354688 | tf_op jit(solution)/shard_map/reduce_sum | solution.py:63
  108.6 4.7 %collective-permute-start.13 = (f32[8,16,1,128]{3,1,0,2:T(8,128)S(1)}, f32[8,16,1,128]{3,1,0,2:T(8,128)S(1)}, u32[]{:S(2)}, u32[]{:S(2)}) collective-permute-start(f32[8,16,1,128]{3,1,0,2:T(8,128)S(1)} %get-tuple-element.534), channel_id=1, source_target_pairs={{4,0},{8,4},{12,8},{16,12},{20,16},{24,20},{28,24},{0,28},{5,1},{9... | collective-permute-start | bytes 196616 | tf_op jit(solution)/shard_map/ppermute | solution.py:29
  138.2 13.0 %multiply_reduce_fusion.3 = (f32[16,16,128]{2,0,1:T(8,128)S(1)}, f32[16,16,128]{2,0,1:T(8,128)S(1)}, f32[16,16,128]{2,0,1:T(8,128)S(1)}, f32[16,16,128]{2,0,1:T(...) fusion(f32[8,16,128]{2,0,1:T(8,128)S(1)} %convert_element_type., ...), kind=kLoop, calls=%fused_computation.298 | loop fusion | flops 30375936 | bytes 13041664 | tf_op jit(solution)/shard_map/jvp()/reduce_sum | solution.py:63
  174.8 4.7 %collective-permute-start.33 = (f32[8,16,1,128]{3,1,0,2:T(8,128)}, f32[8,16,1,128]{3,1,0,2:T(8,128)S(1)}, u32[]{:S(2)}, u32[]{:S(2)}) collective-permute-start(f32[8,16,1,128]{3,1,0,2:T(8,128)} %get-tuple-element.514), channel_id=1, source_target_pairs={{4,0},{8,4},{12,8},{16,12},{20,16},{24,20},{28,24},{0,28},{5,1},{9... | collective-permute-start | bytes 196616 | tf_op jit(solution)/shard_map/ppermute | solution.py:29
  199.6 11.9 %scatter-add.59 = f32[8,16,16,128]{3,1,0,2:T(8,128)} dynamic-update-slice(f32[8,16,16,128]{3,1,0,2:T(8,128)} %scatter-add.56, f32[8,16,16,1]{3,1,0,2:T(8,128)} %slice_add_fusion.6, s32[]{:T(128)} %constant.643.clone.1, s32[]{:T(128)} %constant.643.clone.1, s32[]{:T(128)} %constant.643.clone.1, s32[]{:T(128)} %constant.655.clone.1) | dynamic-update-slice | bytes 16388 | tf_op jit(solution)/shard_map/scatter-add | solution.py:106
  211.6 4.8 %select_reduce_fusion.94 = (f32[16,16,128]{2,0,1:T(8,128)S(1)}, f32[16,16,128]{2,0,1:T(8,128)S(1)}, f32[16,16,128]{2,0,1:T(8,128)S(1)}, f32[16,16,128]{2,0,1:T(8...) fusion(pred[8,16,128]{2,0,1:T(8,128)(4,1)} %get-tuple-element.6, ...), kind=kLoop, calls=%fused_computation.296 | loop fusion | flops 7634944 | bytes 4374528 | tf_op jit(solution)/shard_map/transpose(jvp(jit(_where)))/reduce_sum | solution.py:57
  216.4 4.1 select_reduce_fusion.95
  249.4 4.7 %collective-permute-start.21 = (f32[8,16,128]{2,1,0:T(8,128)}, f32[8,16,128]{2,1,0:T(8,128)}, u32[]{:S(2)}, u32[]{:S(2)}) collective-permute-start(f32[8,16,128]{2,1,0:T(8,128)} %get-tuple-element.365), channel_id=1, source_target_pairs={{0,28},{4,0},{8,4},{12,8},{16,12},{20,16},{24,20},{28,24},{1,29},{... | collective-permute-start | bytes 196616 | tf_op jit(solution)/shard_map/ppermute | solution.py:17
  277.9 4.2 scatter-add.64
  285.0 11.9 %scatter-add.65 = f32[8,16,16,128]{3,1,0,2:T(8,128)} dynamic-update-slice(f32[8,16,16,128]{3,1,0,2:T(8,128)} %scatter-add.64, f32[8,16,16,1]{3,1,0,2:T(8,128)} %slice_add_fusion.4, s32[]{:T(128)} %constant.643.clone.1, s32[]{:T(128)} %constant.643.clone.1, s32[]{:T(128)} %constant.643.clone.1, s32[]{:T(128)} %constant.655.clone.1) | dynamic-update-slice | bytes 16388 | tf_op jit(solution)/shard_map/scatter-add | solution.py:106
  297.0 4.8 %select_reduce_fusion.62 = (f32[16,16,128]{2,0,1:T(8,128)S(1)}, f32[16,16,128]{2,0,1:T(8,128)S(1)}, f32[16,16,128]{2,0,1:T(8,128)S(1)}, f32[16,16,128]{2,0,1:T(8...) fusion(pred[8,16,128]{2,0,1:T(8,128)(4,1)} %get-tuple-element.6, ...), kind=kLoop, calls=%fused_computation.259 | loop fusion | flops 7634944 | bytes 4374528 | tf_op jit(solution)/shard_map/transpose(jvp(jit(_where)))/reduce_sum | solution.py:57
  301.8 4.1 select_reduce_fusion.63
  323.4 10.7 %fusion.127 = f32[8,16,128]{2,0,1:T(8,128)} fusion(f32[8,1,16,128]{3,1,0,2:T(1,128)} %get-tuple-element.516, f32[8,15,16,128]{3,1,0,2:T(8,128)} %get-tuple-element.518, f32[8,15,16,128]{3,1,0,2:T(8,128)} %get-tuple-element.517, f32[8,1,16,128]{3,1,0,2:T(1,128)S(1)} %copy-done.212, f32[8,16,16,128]{3,1,0,2:T(8,128)S(1)} %copy-done.3, ...), kind=kLoop, calls=%fused_computation.154 | loop fusion | flops 21217280 | bytes 8585216 | tf_op jit(solution)/shard_map/transpose(jvp())/reduce_sum | solution.py:69
  336.1 4.5 collective-permute-start.25
  351.9 10.6 %scatter-add.71 = f32[8,16,16,128]{3,1,0,2:T(8,128)S(1)} dynamic-update-slice(f32[8,16,16,128]{3,1,0,2:T(8,128)S(1)} %scatter-add.70, f32[8,16,16,1]{3,1,0,2:T(8,128)S(1)} %slice_add_fusion.2, s32[]{:T(128)} %constant.643.clone.1, s32[]{:T(128)} %constant.643.clone.1, s32[]{:T(128)} %constant.643.clone.1, s32[]{:T(128)} %constant.655.clone.1) | dynamic-update-slice | bytes 16388 | tf_op jit(solution)/shard_map/scatter-add | solution.py:106
  362.5 4.5 select_reduce_fusion.30
  367.0 4.5 select_reduce_fusion.31
  389.1 4.7 %collective-permute-start.29 = (f32[8,16,128]{2,1,0:T(8,128)S(1)}, f32[8,16,128]{2,1,0:T(8,128)S(1)}, u32[]{:S(2)}, u32[]{:S(2)}) collective-permute-start(f32[8,16,128]{2,1,0:T(8,128)S(1)} %get-tuple-element.361), channel_id=1, source_target_pairs={{0,28},{4,0},{8,4},{12,8},{16,12},{20,16},{24,20},{28,24},{1,29},{... | collective-permute-start | bytes 196616 | tf_op jit(solution)/shard_map/ppermute | solution.py:17
  401.9 37.1 %all-reduce.160 = f32[256]{0:T(256)S(1)} all-reduce(f32[256]{0:T(256)S(1)} %bitcast.766), channel_id=2, replica_groups=mesh['gx'=8,'gy'=4] {'gx','gy'}, use_global_device_ids=true, to_apply=%region_140.141.clone | all-reduce | flops 256 | bytes 2048
  450.0 10.6 %scatter-add.79 = f32[8,16,16,128]{3,1,0,2:T(8,128)S(1)} dynamic-update-slice(f32[8,16,16,128]{3,1,0,2:T(8,128)S(1)} %scatter-add.76, f32[8,16,16,1]{3,1,0,2:T(8,128)S(1)} %slice_add_fusion, s32[]{:T(128)} %constant.643.clone.1, s32[]{:T(128)} %constant.643.clone.1, s32[]{:T(128)} %constant.643.clone.1, s32[]{:T(128)} %constant.655.clone.1) | dynamic-update-slice | bytes 16388 | tf_op jit(solution)/shard_map/scatter-add | solution.py:106
  (721 shorter events, 263.2 us)
Async XLA Ops:
  12.8 28.4 %collective-permute-start.4 = (f32[8,16,1,128]{3,1,0,2:T(8,128)}, f32[8,16,1,128]{3,1,0,2:T(8,128)S(1)}, u32[]{:S(2)}, u32[]{:S(2)}) collective-permute-start(f32[8,16,1,128]{3,1,0,2:T(8,128)} %get-tuple-element.545), channel_id=1, source_target_pairs={{0,4},{4,8},{8,12},{12,16},{16,20},{20,24},{24,28},{28,0},{1,5},{5... | collective-permute-start | bytes 196616 | tf_op jit(solution)/shard_map/ppermute | solution.py:26
  15.7 25.4 %collective-permute-start.5 = (f32[8,16,1,128]{3,1,0,2:T(8,128)}, f32[8,16,1,128]{3,1,0,2:T(8,128)S(1)}, u32[]{:S(2)}, u32[]{:S(2)}) collective-permute-start(f32[8,16,1,128]{3,1,0,2:T(8,128)} %get-tuple-element.546), channel_id=1, source_target_pairs={{4,0},{8,4},{12,8},{16,12},{20,16},{24,20},{28,24},{0,28},{5,1},{9... | collective-permute-start | bytes 196616 | tf_op jit(solution)/shard_map/ppermute | solution.py:29
  46.9 8.1 %collective-permute-start.7 = (f32[8,16,18,1]{2,1,3,0:T(8,128)}, f32[8,16,18,1]{2,1,3,0:T(8,128)}, u32[]{:S(2)}, u32[]{:S(2)}) collective-permute-start(f32[8,16,18,1]{2,1,3,0:T(8,128)} %copy.2498), channel_id=1, source_target_pairs={{1,0},{2,1},{3,2},{0,3},{5,4},{6,5},{7,6},{4,7},{9,8},{10,9},{11,1... | collective-permute-start | bytes 27656 | tf_op jit(solution)/shard_map/ppermute | solution.py:29
  83.9 8.4 %collective-permute-start.11 = (f32[8,16,18,1]{2,1,3,0:T(8,128)}, f32[8,16,18,1]{2,1,3,0:T(8,128)}, u32[]{:S(2)}, u32[]{:S(2)}) collective-permute-start(f32[8,16,18,1]{2,1,3,0:T(8,128)} %copy.2502), channel_id=1, source_target_pairs={{1,0},{2,1},{3,2},{0,3},{5,4},{6,5},{7,6},{4,7},{9,8},{10,9},{11,1... | collective-permute-start | bytes 27656 | tf_op jit(solution)/shard_map/ppermute | solution.py:29
  122.4 10.1 %collective-permute-start.15 = (f32[8,16,18,1]{2,1,3,0:T(8,128)S(1)}, f32[8,16,18,1]{2,1,3,0:T(8,128)S(1)}, u32[]{:S(2)}, u32[]{:S(2)}) collective-permute-start(f32[8,16,18,1]{2,1,3,0:T(8,128)S(1)} %copy.2506), channel_id=1, source_target_pairs={{1,0},{2,1},{3,2},{0,3},{5,4},{6,5},{7,6},{4,7},{9,8},{10,9},{11,1... | collective-permute-start | bytes 27656 | tf_op jit(solution)/shard_map/ppermute | solution.py:29
  160.9 26.2 %collective-permute-start.16 = (f32[8,16,128]{2,1,0:T(8,128)}, f32[8,16,128]{2,1,0:T(8,128)}, u32[]{:S(2)}, u32[]{:S(2)}) collective-permute-start(f32[8,16,128]{2,1,0:T(8,128)} %get-tuple-element.368), channel_id=1, source_target_pairs={{0,4},{4,8},{8,12},{12,16},{16,20},{20,24},{24,28},{28,0},{1,5},{5... | collective-permute-start | bytes 196616 | tf_op jit(solution)/shard_map/ppermute | solution.py:17
  165.7 13.8 %collective-permute-start.18 = (f32[8,16,16]{2,1,0:T(8,128)}, f32[8,16,16]{2,1,0:T(8,128)}, u32[]{:S(2)}, u32[]{:S(2)}) collective-permute-start(f32[8,16,16]{2,1,0:T(8,128)} %bitcast.200), channel_id=1, source_target_pairs={{0,1},{1,2},{2,3},{3,0},{4,5},{5,6},{6,7},{7,4},{8,9},{9,10},{10,1... | collective-permute-start | bytes 24584 | tf_op jit(solution)/shard_map/ppermute | solution.py:17
  168.4 16.0 %collective-permute-start.19 = (f32[8,16,16]{2,1,0:T(8,128)}, f32[8,16,16]{2,1,0:T(8,128)}, u32[]{:S(2)}, u32[]{:S(2)}) collective-permute-start(f32[8,16,16]{2,1,0:T(8,128)} %bitcast.202), channel_id=1, source_target_pairs={{0,3},{1,0},{2,1},{3,2},{4,7},{5,4},{6,5},{7,6},{8,11},{9,8},{10,9... | collective-permute-start | bytes 24584 | tf_op jit(solution)/shard_map/ppermute | solution.py:17
  174.8 55.5 %collective-permute-start.32 = (f32[8,16,1,128]{3,1,0,2:T(8,128)}, f32[8,16,1,128]{3,1,0,2:T(8,128)S(1)}, u32[]{:S(2)}, u32[]{:S(2)}) collective-permute-start(f32[8,16,1,128]{3,1,0,2:T(8,128)} %get-tuple-element.513), channel_id=1, source_target_pairs={{0,4},{4,8},{8,12},{12,16},{16,20},{20,24},{24,28},{28,0},{1,5},{5... | collective-permute-start | bytes 196616 | tf_op jit(solution)/shard_map/ppermute | solution.py:26
  174.8 55.5 %collective-permute-start.33 = (f32[8,16,1,128]{3,1,0,2:T(8,128)}, f32[8,16,1,128]{3,1,0,2:T(8,128)S(1)}, u32[]{:S(2)}, u32[]{:S(2)}) collective-permute-start(f32[8,16,1,128]{3,1,0,2:T(8,128)} %get-tuple-element.514), channel_id=1, source_target_pairs={{4,0},{8,4},{12,8},{16,12},{20,16},{24,20},{28,24},{0,28},{5,1},{9... | collective-permute-start | bytes 196616 | tf_op jit(solution)/shard_map/ppermute | solution.py:29
  179.6 9.4 %collective-permute-start.17 = (f32[8,16,128]{2,1,0:T(8,128)}, f32[8,16,128]{2,1,0:T(8,128)}, u32[]{:S(2)}, u32[]{:S(2)}) collective-permute-start(f32[8,16,128]{2,1,0:T(8,128)} %get-tuple-element.367), channel_id=1, source_target_pairs={{0,28},{4,0},{8,4},{12,8},{16,12},{20,16},{24,20},{28,24},{1,29},{... | collective-permute-start | bytes 196616 | tf_op jit(solution)/shard_map/ppermute | solution.py:17
  235.5 24.1 %collective-permute-start.34 = (f32[8,16,18,1]{2,1,3,0:T(8,128)}, f32[8,16,18,1]{2,1,3,0:T(8,128)}, u32[]{:S(2)}, u32[]{:S(2)}) collective-permute-start(f32[8,16,18,1]{2,1,3,0:T(8,128)} %copy.2524), channel_id=1, source_target_pairs={{0,1},{1,2},{2,3},{3,0},{4,5},{5,6},{6,7},{7,4},{8,9},{9,10},{10,1... | collective-permute-start | bytes 27656 | tf_op jit(solution)/shard_map/ppermute | solution.py:26
  238.7 27.3 %collective-permute-start.35 = (f32[8,16,18,1]{2,1,3,0:T(8,128)}, f32[8,16,18,1]{2,1,3,0:T(8,128)}, u32[]{:S(2)}, u32[]{:S(2)}) collective-permute-start(f32[8,16,18,1]{2,1,3,0:T(8,128)} %copy.2526), channel_id=1, source_target_pairs={{1,0},{2,1},{3,2},{0,3},{5,4},{6,5},{7,6},{4,7},{9,8},{10,9},{11,1... | collective-permute-start | bytes 27656 | tf_op jit(solution)/shard_map/ppermute | solution.py:29
  240.4 33.4 %collective-permute-start.20 = (f32[8,16,128]{2,1,0:T(8,128)}, f32[8,16,128]{2,1,0:T(8,128)}, u32[]{:S(2)}, u32[]{:S(2)}) collective-permute-start(f32[8,16,128]{2,1,0:T(8,128)} %get-tuple-element.366), channel_id=1, source_target_pairs={{0,4},{4,8},{8,12},{12,16},{16,20},{20,24},{24,28},{28,0},{1,5},{5... | collective-permute-start | bytes 196616 | tf_op jit(solution)/shard_map/ppermute | solution.py:17
  245.8 11.1 %collective-permute-start.23 = (f32[8,16,16]{2,1,0:T(8,128)}, f32[8,16,16]{2,1,0:T(8,128)}, u32[]{:S(2)}, u32[]{:S(2)}) collective-permute-start(f32[8,16,16]{2,1,0:T(8,128)} %bitcast.753), channel_id=1, source_target_pairs={{0,3},{1,0},{2,1},{3,2},{4,7},{5,4},{6,5},{7,6},{8,11},{9,8},{10,9... | collective-permute-start | bytes 24584 | tf_op jit(solution)/shard_map/ppermute | solution.py:17
  249.4 25.6 %collective-permute-start.21 = (f32[8,16,128]{2,1,0:T(8,128)}, f32[8,16,128]{2,1,0:T(8,128)}, u32[]{:S(2)}, u32[]{:S(2)}) collective-permute-start(f32[8,16,128]{2,1,0:T(8,128)} %get-tuple-element.365), channel_id=1, source_target_pairs={{0,28},{4,0},{8,4},{12,8},{16,12},{20,16},{24,20},{28,24},{1,29},{... | collective-permute-start | bytes 196616 | tf_op jit(solution)/shard_map/ppermute | solution.py:17
  314.0 32.1 %collective-permute-start.24 = (f32[8,16,128]{2,1,0:T(8,128)}, f32[8,16,128]{2,1,0:T(8,128)}, u32[]{:S(2)}, u32[]{:S(2)}) collective-permute-start(f32[8,16,128]{2,1,0:T(8,128)} %get-tuple-element.364), channel_id=1, source_target_pairs={{0,4},{4,8},{8,12},{12,16},{16,20},{20,24},{24,28},{28,0},{1,5},{5... | collective-permute-start | bytes 196616 | tf_op jit(solution)/shard_map/ppermute | solution.py:17
  318.9 21.7 %collective-permute-start.26 = (f32[8,16,16]{2,1,0:T(8,128)}, f32[8,16,16]{2,1,0:T(8,128)}, u32[]{:S(2)}, u32[]{:S(2)}) collective-permute-start(f32[8,16,16]{2,1,0:T(8,128)} %bitcast.751), channel_id=1, source_target_pairs={{0,1},{1,2},{2,3},{3,0},{4,5},{5,6},{6,7},{7,4},{8,9},{9,10},{10,1... | collective-permute-start | bytes 24584 | tf_op jit(solution)/shard_map/ppermute | solution.py:17
  321.6 21.8 %collective-permute-start.27 = (f32[8,16,16]{2,1,0:T(8,128)}, f32[8,16,16]{2,1,0:T(8,128)}, u32[]{:S(2)}, u32[]{:S(2)}) collective-permute-start(f32[8,16,16]{2,1,0:T(8,128)} %bitcast.752), channel_id=1, source_target_pairs={{0,3},{1,0},{2,1},{3,2},{4,7},{5,4},{6,5},{7,6},{8,11},{9,8},{10,9... | collective-permute-start | bytes 24584 | tf_op jit(solution)/shard_map/ppermute | solution.py:17
  336.1 11.2 %collective-permute-start.25 = (f32[8,16,128]{2,1,0:T(8,128)}, f32[8,16,128]{2,1,0:T(8,128)}, u32[]{:S(2)}, u32[]{:S(2)}) collective-permute-start(f32[8,16,128]{2,1,0:T(8,128)} %get-tuple-element.363), channel_id=1, source_target_pairs={{0,28},{4,0},{8,4},{12,8},{16,12},{20,16},{24,20},{28,24},{1,29},{... | collective-permute-start | bytes 196616 | tf_op jit(solution)/shard_map/ppermute | solution.py:17
  389.1 55.9 %collective-permute-start.28 = (f32[8,16,128]{2,1,0:T(8,128)S(1)}, f32[8,16,128]{2,1,0:T(8,128)S(1)}, u32[]{:S(2)}, u32[]{:S(2)}) collective-permute-start(f32[8,16,128]{2,1,0:T(8,128)S(1)} %get-tuple-element.362), channel_id=1, source_target_pairs={{0,4},{4,8},{8,12},{12,16},{16,20},{20,24},{24,28},{28,0},{1,5},{5... | collective-permute-start | bytes 196616 | tf_op jit(solution)/shard_map/ppermute | solution.py:17
  389.1 57.0 %collective-permute-start.29 = (f32[8,16,128]{2,1,0:T(8,128)S(1)}, f32[8,16,128]{2,1,0:T(8,128)S(1)}, u32[]{:S(2)}, u32[]{:S(2)}) collective-permute-start(f32[8,16,128]{2,1,0:T(8,128)S(1)} %get-tuple-element.361), channel_id=1, source_target_pairs={{0,28},{4,0},{8,4},{12,8},{16,12},{20,16},{24,20},{28,24},{1,29},{... | collective-permute-start | bytes 196616 | tf_op jit(solution)/shard_map/ppermute | solution.py:17
  395.9 43.7 %collective-permute-start.30 = (f32[8,16,16]{2,1,0:T(8,128)S(1)}, f32[8,16,16]{2,1,0:T(8,128)}, u32[]{:S(2)}, u32[]{:S(2)}) collective-permute-start(f32[8,16,16]{2,1,0:T(8,128)S(1)} %bitcast.754), channel_id=1, source_target_pairs={{0,1},{1,2},{2,3},{3,0},{4,5},{5,6},{6,7},{7,4},{8,9},{9,10},{10,1... | collective-permute-start | bytes 24584 | tf_op jit(solution)/shard_map/ppermute | solution.py:17
  398.6 43.7 %collective-permute-start.31 = (f32[8,16,16]{2,1,0:T(8,128)}, f32[8,16,16]{2,1,0:T(8,128)}, u32[]{:S(2)}, u32[]{:S(2)}) collective-permute-start(f32[8,16,16]{2,1,0:T(8,128)} %bitcast.755), channel_id=1, source_target_pairs={{0,3},{1,0},{2,1},{3,2},{4,7},{5,4},{6,5},{7,6},{8,11},{9,8},{10,9... | collective-permute-start | bytes 24584 | tf_op jit(solution)/shard_map/ppermute | solution.py:17
  (251 other events, 852.8 us)
where the time goes:
time: 471 us; the launch traced here: 463 us
  local copies, waits for them, and re-layouts  192 us (41%)
  other arithmetic  147 us (31%)
  starting transfers between devices  57.4 us (12%)
  blocking collectives  37.1 us (8%)
  matrix products  18 us (4%)
  waiting for transfers between devices  6.38 us (1%)
  between operations  5.23 us (1%)
    scatter-add x8, local copies, waits for them, and re-layouts, return_rims(): inner = inner.at[:, :, :, 0 if by == 1 else cols - 1].add(arrived)  57.1 us
    unnamed x1, blocking collectives  37.1 us
    reduce_sum x4, other arithmetic, update_fractions(): occupied = jnp.sum(centre * present_crystals[:, None], axis=0)  34.2 us
    reduce_sum x7, other arithmetic, update_fractions(): jnp.where(crystal_equality[index][:, slot][:, None], beside[slot][None],...  31.3 us
    ppermute x10, starting transfers between devices, padded(): lax.ppermute(lax.slice_in_dim(block, 0, width, axis=dim), axis, backward)  30.1 us
    slice x12, local copies, waits for them, and re-layouts, return_rims(): face = cycle_cot[:, :, 1:rows + 1, cols + 1 if by == 1 else 0]  28.1 us
    broadcast_in_dim x24, other arithmetic, update_fractions(): jnp.where(crystal_equality[index][:, slot][:, None], beside[slot][None],...  26.2 us
    ppermute x16, starting transfers between devices, passed_along(): return lax.ppermute(x, axis, [(i, (i + by) % count) for i in range(count)])  23.3 us
  transfers between devices with their start and end apart: 36, of which 4 were waited for; matrix products, arithmetic and copies ran while one was open for 37% of the time, Pallas kernels for 0%

commit v1 on v0

v1 whole, which is shorter than its diff:
```python
import functools

import jax
import jax.numpy as jnp
from jax import lax
from jax.experimental import pallas as pl
from jax.experimental.pallas import tpu as pltpu
from jax.sharding import PartitionSpec as P

STEPS = 4
MESH = pl.DeviceIdType.MESH
LANES = 128
EXCHANGES = 7


def take_rows(values, index):
    return jnp.take_along_axis(values, index, axis=0)


def lookup(tables, ids):
    row = lax.shift_right_logical(ids, 7)
    col = lax.bitwise_and(ids, 127)
    found = None
    for r, table in enumerate(tables):
        got = jnp.take_along_axis(table, col, axis=1)
        found = got if found is None else jnp.where(row == r, got, found)
    return found


def kernel(
    nx, ny, slots, depth, rows, out_per,
    therm, sf, seed, ids, counts, mob, opos,
    out, gout,
    p0, p1, p2, p3, a4, a3, a2, a1, drive0, seed32,
    live, index, match, moba, act, pos, gacc, ones,
    xh, ye, yh, hc, le, lxh, lyh,
    gs, g3, r1, s2, r2,
    xs_sem, xr_sem, ys_sem, yr_sem, ls_sem, lr_sem, s1_sem, q1_sem, s2_sem, q2_sem,
):
    gx = lax.axis_index("gx")
    gy = lax.axis_index("gy")
    ndev = nx * ny
    per = LANES // (2 * depth)
    packs = rows // per
    stride = depth * rows
    phases = (p0, p1, p2, p3)
    adjoints = {4: a4, 3: a3, 2: a2, 1: a1}

    barrier = pltpu.get_barrier_semaphore()
    for o in range(1, nx):
        pl.semaphore_signal(barrier, inc=1, device_id=(lax.rem(gx + o, nx), gy), device_id_type=MESH)
    for o in range(1, ny):
        pl.semaphore_signal(barrier, inc=1, device_id=(gx, lax.rem(gy + o, ny)), device_id_type=MESH)

    low_x = (lax.rem(gx + nx - 1, nx), gy)
    high_x = (lax.rem(gx + 1, nx), gy)
    low_y = (gx, lax.rem(gy + ny - 1, ny))
    high_y = (gx, lax.rem(gy + 1, ny))

    lane = lax.broadcasted_iota(jnp.int32, (slots, LANES), 1)
    sub = lax.broadcasted_iota(jnp.int32, (slots, LANES), 0)
    pair = lax.shift_right_logical(lane, 1)
    group = lane // (2 * depth)
    first = lane == 0
    final = lane == LANES - 1
    even = lax.bitwise_and(lane, 1) == 0

    def x_copies(e, src):
        return (
            pltpu.make_async_remote_copy(
                src_ref=src.at[rows - 1], dst_ref=xh.at[e, 0], send_sem=xs_sem.at[e, 0],
                recv_sem=xr_sem.at[e, 0], device_id=high_x, device_id_type=MESH),
            pltpu.make_async_remote_copy(
                src_ref=src.at[0], dst_ref=xh.at[e, 1], send_sem=xs_sem.at[e, 1],
                recv_sem=xr_sem.at[e, 1], device_id=low_x, device_id_type=MESH),
        )

    def y_copies(e):
        return (
            pltpu.make_async_remote_copy(
                src_ref=ye.at[e], dst_ref=yh.at[e, 0], send_sem=ys_sem.at[e, 0],
                recv_sem=yr_sem.at[e, 0], device_id=high_y, device_id_type=MESH),
            pltpu.make_async_remote_copy(
                src_ref=ye.at[e], dst_ref=yh.at[e, 1], send_sem=ys_sem.at[e, 1],
                recv_sem=yr_sem.at[e, 1], device_id=low_y, device_id_type=MESH),
        )

    def swap_sides(from_low, from_high):
        return jnp.where(even, pltpu.roll(from_high, LANES - 1, 1), pltpu.roll(from_low, 1, 1))

    def pack_row(e, x, values):
        packed = jnp.zeros((slots, LANES), jnp.float32)
        for z, value in enumerate(values):
            packed = jnp.where(pair == z, pltpu.roll(value, 2 * z + 1, 1), packed)
        part = lax.rem(x, per)
        packed = pltpu.roll(packed, part * (2 * depth), 1)
        ye[e, x // per] = jnp.where(group == part, packed, ye[e, x // per])

    mob_tables = [jnp.broadcast_to(mob[r : r + 1, :], (slots, LANES)) for r in range(mob.shape[0])]
    pos_tables = [jnp.broadcast_to(opos[r : r + 1, :], (slots, LANES)) for r in range(opos.shape[0])]
    edge = jnp.zeros((slots, LANES), jnp.int32)
    for x in range(rows):
        own = ids[pl.ds(x, slots, stride=rows), :]
        alive = sub < jnp.broadcast_to(counts[x : x + 1, :], (slots, LANES))
        here = jnp.where(alive, own, -1)
        live[x + 1] = here
        edge = jnp.where(pair == x, pltpu.roll(here, 2 * x + 1, 1), edge)
        active = jnp.where(alive, 1.0, 0.0)
        act[x] = active
        moba[x] = 0.05 * active * lookup(mob_tables, own)
        pos[x] = lookup(pos_tables, own)
        gacc[x] = jnp.zeros((slots, LANES), jnp.float32)
    le[...] = edge
    ye[...] = jnp.zeros(ye.shape, jnp.float32)
    span = slots * depth
    ones[...] = jnp.where(
        lax.broadcasted_iota(jnp.int32, (span, span), 0) // slots
        == lax.broadcasted_iota(jnp.int32, (span, span), 1) // slots,
        0.25, 0.0,
    ).astype(jnp.bfloat16)

    def load_phase(x, carry):
        active = act[x]
        values = []
        for z in range(depth):
            value = sf[pl.ds(z * rows + x, slots, stride=stride), :] * active
            p0[x, z] = value
            values.append(value)
        pack_row(0, x, values)
        return carry

    lax.fori_loop(0, rows, load_phase, 0)

    pl.semaphore_wait(barrier, (nx - 1) + (ny - 1))
    id_copies = (
        pltpu.make_async_remote_copy(
            src_ref=live.at[rows], dst_ref=lxh.at[0], send_sem=ls_sem.at[0],
            recv_sem=lr_sem.at[0], device_id=high_x, device_id_type=MESH),
        pltpu.make_async_remote_copy(
            src_ref=live.at[1], dst_ref=lxh.at[1], send_sem=ls_sem.at[1],
            recv_sem=lr_sem.at[1], device_id=low_x, device_id_type=MESH),
        pltpu.make_async_remote_copy(
            src_ref=le, dst_ref=lyh.at[0], send_sem=ls_sem.at[2],
            recv_sem=lr_sem.at[2], device_id=high_y, device_id_type=MESH),
        pltpu.make_async_remote_copy(
            src_ref=le, dst_ref=lyh.at[1], send_sem=ls_sem.at[3],
            recv_sem=lr_sem.at[3], device_id=low_y, device_id_type=MESH),
    )
    sent = list(id_copies)

    def launch(e, src):
        xc, yc = x_copies(e, src), y_copies(e)
        for c in yc + xc:
            c.start()
            sent.append(c)
        return xc, yc

    for c in id_copies:
        c.start()
    flight = {0: launch(0, p0)}

    def widen(i, carry):
        block = pl.ds(pl.multiple_of(i * 128, 128), 128)
        seed32[block, :] = seed[block, :].astype(jnp.float32)
        return carry

    lax.fori_loop(0, seed.shape[0] // 128, widen, 0)

    def load_seed(x, carry):
        active = act[x]
        values = []
        for z in range(depth):
            value = seed32[pl.ds(z * rows + x, slots, stride=stride), :] * active
            a4[x, z] = value
            values.append(value)
        pack_row(3, x, values)
        return carry

    lax.fori_loop(0, rows, load_seed, 0)
    flight[3] = launch(3, a4)

    for c in id_copies:
        c.wait_recv()
    live[0] = lxh[0]
    live[rows + 1] = lxh[1]
    id_sides = swap_sides(lyh[0], lyh[1])

    def match_row(x, carry):
        own = live[x + 1]
        side = pltpu.roll(id_sides, LANES - 1 - 2 * x, 1)
        beside = (
            live[x],
            live[x + 2],
            jnp.where(first, side, pltpu.roll(own, 1, 1)),
            jnp.where(final, side, pltpu.roll(own, LANES - 1, 1)),
        )
        for n, other in enumerate(beside):
            where = jnp.zeros((slots, LANES), jnp.int32)
            hit = jnp.zeros((slots, LANES), jnp.float32)
            for j in range(slots):
                same = own == jnp.broadcast_to(other[j : j + 1, :], (slots, LANES))
                where = jnp.where(same, j, where)
                hit = jnp.where(same, 1.0, hit)
            index[n, x] = where
            match[n, x] = hit
        return carry

    lax.fori_loop(0, rows, match_row, 0)

    def open_sides(e):
        for c in flight[e][1]:
            c.wait_recv()
        for i in range(packs):
            hc[e, i] = swap_sides(yh[e, 0, i], yh[e, 1, i])

    def lateral(e, x, centre, up, down):
        part = lax.rem(x, per)
        side_row = pltpu.roll(hc[e, x // per], lax.rem(LANES - part * (2 * depth), LANES), 1)
        where = [index[n, x] for n in range(4)]
        hit = [match[n, x] for n in range(4)]
        totals = []
        for z in range(depth):
            c = centre[z]
            side = pltpu.roll(side_row, LANES - 1 - 2 * z, 1)
            left = jnp.where(first, side, pltpu.roll(c, 1, 1))
            right = jnp.where(final, side, pltpu.roll(c, LANES - 1, 1))
            total = (
                take_rows(up(z), where[0]) * hit[0]
                + take_rows(down(z), where[1]) * hit[1]
                + take_rows(left, where[2]) * hit[2]
                + take_rows(right, where[3]) * hit[3]
            )
            total = total + centre[min(z + 1, depth - 1)] + centre[max(z - 1, 0)]
            totals.append(total)
        return totals

    def slot_sums(values):
        stacked = jnp.concatenate(values, axis=0).astype(jnp.bfloat16)
        sums = jnp.dot(ones[...], stacked, preferred_element_type=jnp.float32)
        return [sums[z * slots : (z + 1) * slots] for z in range(depth)]

    def forward_row(s, x, up, down):
        src, dst = phases[s], phases[s + 1]
        centre = [src[x, z] for z in range(depth)]
        rate = therm[s] * moba[x]
        crowd = slot_sums(centre)
        totals = lateral(s, x, centre, up, down)
        values = []
        for z in range(depth):
            c = centre[z]
            drive = totals[z] + c * ((1.75 - c) * c - (6.5 + crowd[z]))
            if s == 0:
                drive0[x, z] = drive
            value = c + rate * drive
            dst[x, z] = value
            values.append(value)
        if s + 1 < STEPS - 1:
            pack_row(s + 1, x, values)

    def backward_row(s, x, up, down):
        src, phase = adjoints[s + 1], phases[s]
        e = 3 + (STEPS - 1 - s)
        active = act[x]
        rate = therm[s] * moba[x]
        centre = [src[x, z] for z in range(depth)]
        c = [phase[x, z] for z in range(depth)]
        crowd = slot_sums(c)
        shared = slot_sums([rate * centre[z] * c[z] for z in range(depth)])
        totals = lateral(e, x, centre, up, down)
        values = []
        now = jnp.zeros((slots, LANES), jnp.float32)
        before = jnp.zeros((slots, LANES), jnp.float32)
        for z in range(depth):
            a = centre[z]
            spread = totals[z] - 6.0 * a
            local = (3.5 - 3.0 * c[z]) * c[z] - (0.5 + crowd[z])
            value = a + rate * (spread + a * local) - active * shared[z]
            if s > 0:
                adjoints[s][x, z] = value
                values.append(value)
                now = now + c[z] * (spread + a * ((1.75 - c[z]) * c[z] - (0.5 + crowd[z])))
                if s == 1:
                    before = before + value * drive0[x, z]
            else:
                out[pl.ds(z * rows + x, slots, stride=stride), :] = value
        if s > 0:
            gained = gacc[x] + therm[s] * now
            if s == 1:
                gained = gained + therm[0] * before
            gacc[x] = gained
            pack_row(e + 1, x, values)

    def inner(row, s, src):
        def body(x, carry):
            row(s, x, lambda z: src[x - 1, z], lambda z: src[x + 1, z])
            return carry

        lax.fori_loop(1, rows - 1, body, 0)

    def rim(row, s, src, e):
        for c in flight[e][0]:
            c.wait_recv()

        def top(z):
            return xh[e, 0, z]

        def bottom(z):
            return xh[e, 1, z]

        def body(i, carry):
            x = i * (rows - 1)
            low = i == 0

            def up(z):
                return jnp.where(low, xh[e, 0, z], src[rows - 2, z])

            def down(z):
                return jnp.where(low, src[1, z], xh[e, 1, z])

            row(s, x, up, down)
            return carry

        lax.fori_loop(0, 2, body, 0)

    for s in range(STEPS - 1):
        open_sides(s)
        inner(forward_row, s, phases[s])
        rim(forward_row, s, phases[s], s)
        if s + 1 < STEPS - 1:
            flight[s + 1] = launch(s + 1, phases[s + 1])

    for s in range(STEPS - 1, 0, -1):
        e = 3 + (STEPS - 1 - s)
        open_sides(e)
        inner(backward_row, s, adjoints[s + 1])
        rim(backward_row, s, adjoints[s + 1], e)
        flight[e + 1] = launch(e + 1, adjoints[s])

    which = lax.broadcasted_iota(jnp.int32, (ndev, LANES), 0)

    def gather_grains(x, total):
        value = 0.05 * gacc[x]
        spot = pos[x]
        owner = spot // out_per
        place = spot - owner * out_per
        picks, terms = [], []
        for k in range(slots):
            picks.append(jnp.where(which == jnp.broadcast_to(owner[k : k + 1, :], (ndev, LANES)), 1.0, 0.0))
            term = jnp.where(
                sub == jnp.broadcast_to(place[k : k + 1, :], (slots, LANES)),
                jnp.broadcast_to(value[k : k + 1, :], (slots, LANES)), 0.0)
            coarse = term.astype(jnp.bfloat16).astype(jnp.float32)
            terms.append(jnp.concatenate([coarse, term - coarse], axis=0))
        pick = jnp.concatenate(picks, axis=1).astype(jnp.bfloat16)
        term = jnp.concatenate(terms, axis=1).astype(jnp.bfloat16)
        return total + lax.dot_general(
            pick, term, (((1,), (1,)), ((), ())), preferred_element_type=jnp.float32)

    total = lax.fori_loop(0, rows, gather_grains, jnp.zeros((ndev, 2 * slots), jnp.float32))
    gs[...] = jnp.zeros(gs.shape, jnp.float32)
    gs[:, 0 : 2 * slots] = total
    for d in range(ndev):
        g3[d] = gs[d : d + 1, :]
    stage1 = []
    for o in range(1, nx):
        to = lax.rem(gx + o, nx)
        c = pltpu.make_async_remote_copy(
            src_ref=g3.at[pl.ds(to * ny, ny)], dst_ref=r1.at[o], send_sem=s1_sem.at[o],
            recv_sem=q1_sem.at[o], device_id=(to, gy), device_id_type=MESH)
        c.start()
        stage1.append(c)
        sent.append(c)

    open_sides(EXCHANGES - 1)
    inner(backward_row, 0, a1)

    for c in stage1:
        c.wait_recv()
    summed = g3[pl.ds(gx * ny, ny)]
    for o in range(1, nx):
        summed = summed + r1[o]
    s2[...] = summed
    stage2 = []
    for o in range(1, ny):
        to = lax.rem(gy + o, ny)
        c = pltpu.make_async_remote_copy(
            src_ref=s2.at[to], dst_ref=r2.at[o], send_sem=s2_sem.at[o],
            recv_sem=q2_sem.at[o], device_id=(gx, to), device_id_type=MESH)
        c.start()
        stage2.append(c)
        sent.append(c)

    rim(backward_row, 0, a1, EXCHANGES - 1)

    for c in stage2:
        c.wait_recv()
    whole = s2[gy]
    for o in range(1, ny):
        whole = whole + r2[o]
    gout[...] = whole + pltpu.roll(whole, LANES - slots, 1)
    for c in sent:
        c.wait_send()


def shards(
    nx, ny,
    saved_fractions, adjoint_seed, slot_ids, active_counts, mobility, owner_pos, saved_instant
):
    slots, depth, rows, cols = saved_fractions.shape
    grains = mobility.shape[0]
    ndev = nx * ny
    out_per = grains // ndev
    steps = jnp.arange(STEPS, dtype=jnp.float32)
    therm = 0.75 + 0.5 * jnp.cos(0.3 * (saved_instant[0].astype(jnp.float32) + steps))
    flat = slots * depth * rows
    block = pltpu.VMEM((rows, depth, slots, cols), jnp.float32)
    plane = pltpu.VMEM((rows, slots, cols), jnp.float32)
    packs = rows * 2 * depth // LANES
    dma = pltpu.SemaphoreType.DMA
    vmem = pl.BlockSpec(memory_space=pltpu.VMEM)
    adjoint, owned = pl.pallas_call(
        functools.partial(kernel, nx, ny, slots, depth, rows, out_per),
        out_shape=(
            jax.ShapeDtypeStruct((flat, cols), jnp.float32),
            jax.ShapeDtypeStruct((1, LANES), jnp.float32),
        ),
        in_specs=[pl.BlockSpec(memory_space=pltpu.SMEM)] + [vmem] * 6,
        out_specs=(vmem, vmem),
        scratch_shapes=[block] * 9 + [
            pltpu.VMEM((flat, cols), jnp.float32),
            pltpu.VMEM((rows + 2, slots, cols), jnp.int32),
            pltpu.VMEM((4, rows, slots, cols), jnp.int32),
            pltpu.VMEM((4, rows, slots, cols), jnp.float32),
            plane, plane,
            pltpu.VMEM((rows, slots, cols), jnp.int32),
            plane,
            pltpu.VMEM((slots * depth, slots * depth), jnp.bfloat16),
            pltpu.VMEM((EXCHANGES, 2, depth, slots, cols), jnp.float32),
            pltpu.VMEM((EXCHANGES, packs, slots, LANES), jnp.float32),
            pltpu.VMEM((EXCHANGES, 2, packs, slots, LANES), jnp.float32),
            pltpu.VMEM((EXCHANGES, packs, slots, LANES), jnp.float32),
            pltpu.VMEM((slots, LANES), jnp.int32),
            pltpu.VMEM((2, slots, LANES), jnp.int32),
            pltpu.VMEM((2, slots, LANES), jnp.int32),
            pltpu.VMEM((ndev, LANES), jnp.float32),
            pltpu.VMEM((ndev, 1, LANES), jnp.float32),
            pltpu.VMEM((nx, ny, 1, LANES), jnp.float32),
            pltpu.VMEM((ny, 1, LANES), jnp.float32),
            pltpu.VMEM((ny, 1, LANES), jnp.float32),
            dma((EXCHANGES, 2)), dma((EXCHANGES, 2)),
            dma((EXCHANGES, 2)), dma((EXCHANGES, 2)),
            dma((4,)), dma((4,)),
            dma((nx,)), dma((nx,)), dma((ny,)), dma((ny,)),
        ],
        compiler_params=pltpu.CompilerParams(
            collective_id=0, has_side_effects=True, vmem_limit_bytes=48 * 1024 * 1024
        ),
    )(
        therm,
        saved_fractions.reshape(flat, cols),
        adjoint_seed.reshape(flat, cols),
        slot_ids.reshape(slots * rows, cols),
        active_counts,
        mobility.reshape(grains // LANES, LANES),
        owner_pos.reshape(grains // LANES, LANES),
    )
    return adjoint.reshape(saved_fractions.shape), owned[0, :out_per]


def solution(mesh):
    placed = (
        P(None, None, "gx", "gy"),
        P(None, None, "gx", "gy"),
        P(None, "gx", "gy"),
        P("gx", "gy"),
        P(),
        P(),
        P(),
    )
    return jax.shard_map(
        functools.partial(shards, mesh.shape["gx"], mesh.shape["gy"]),
        mesh=mesh,
        in_specs=placed,
        out_specs=(P(None, None, "gx", "gy"), P(("gx", "gy"))),
        check_vma=False,
    )
```

time: 471 us -> 69.3 us (0.15); the launches traced: 463 us -> 69 us
  local copies, waits for them, and re-layouts: 192 us -> 5.27 us
  other arithmetic: 147 us -> 0.05 us
  Pallas kernels: 0 us -> 62.3 us
  starting transfers between devices: 57.4 us -> 0 us
  blocking collectives: 37.1 us -> 0 us
  matrix products: 18 us -> 0 us
  waiting for transfers between devices: 6.38 us -> 0 us
    reduce_sum x15 -> x0, other arithmetic: 81.4 us -> none  [the longest x4 34.2 us: update_fractions(): occupied = jnp.sum(centre * present_crystals[:, None], axis=0)]
    slice x46 -> x0, local copies, waits for them, and re-layouts: 71.5 us -> none  [the longest x12 28.1 us: return_rims(): face = cycle_cot[:, :, 1:rows + 1, cols + 1 if by == 1 else 0]]
    pallas_call x0 -> x1, Pallas kernels: none -> 62.3 us  [shards(): pl.pallas_call(functools.partial(kernel, nx, ny, slots, depth, rows, out_...]
    ppermute x36 -> x0, starting transfers between devices: 57.4 us -> none  [the longest x10 30.1 us: padded(): lax.ppermute(lax.slice_in_dim(block, 0, width, axis=dim), axis, backward)]
    scatter-add x8 -> x0, local copies, waits for them, and re-layouts: 57.1 us -> none  [return_rims(): inner = inner.at[:, :, :, 0 if by == 1 else cols - 1].add(arrived)]
    unnamed x1 -> x0, blocking collectives: 37.1 us -> none
    broadcast_in_dim x24 -> x0, other arithmetic: 26.2 us -> none  [update_fractions(): jnp.where(crystal_equality[index][:, slot][:, None], beside[slot][None],...]
    another operation x9 -> x0, local copies, waits for them, and re-layouts: 22.2 us -> none
  transfers between devices with their start and end apart: 36 -> 0, of which waited for: 4 -> 0; matrix products, arithmetic and copies ran while one was open for 37% -> 0% of each run, Pallas kernels for 0% -> 0%
where the time goes in v1:
time: 69.3 us; the launch traced here: 69 us
  Pallas kernels  62.3 us (90%)
  local copies, waits for them, and re-layouts  5.27 us (8%)
  between operations  1.31 us (2%)
    pallas_call x1, Pallas kernels, shards(): pl.pallas_call(functools.partial(kernel, nx, ny, slots, depth, rows, out_...  62.3 us
    unnamed x13, local copies, waits for them, and re-layouts  4.76 us

profile of v1, /device:TPU:0, one launch (start us, length us, event | category | flops | bytes accessed | tf_op | source)
XLA Modules:
  0.0 69.0 jit_solution(16049821327182561361)
XLA Ops:
  1.3 0.0 copy-start.3
  1.3 0.0 copy-start.5
  1.3 0.0 copy-start.4
  1.4 0.6 copy-done.3
  2.0 0.0 copy-done.5
  2.0 0.0 copy-done.4
  2.0 0.0 copy-start
  2.0 1.2 %copy-done = f32[8,16,16,128]{3,2,1,0:T(8,128)S(1)} copy-done((f32[8,16,16,128]{3,2,1,0:T(8,128)S(1)}, f32[8,16,16,128]{3,2,1,0:T(8,128)}, u32[]{:S(2)}) %copy-start) | copy-done | bytes 1048600
  3.3 0.0 copy-start.1
  3.3 1.0 %copy-done.1 = bf16[8,16,16,128]{3,2,1,0:T(8,128)(2,1)S(1)} copy-done((bf16[8,16,16,128]{3,2,1,0:T(8,128)(2,1)S(1)}, bf16[8,16,16,128]{3,2,1,0:T(8,128)(2,1)}, u32[]{:S(2)}) %copy-start.1) | copy-done | bytes 524312
  4.3 0.0 copy-start.2
  4.3 0.8 %copy-done.2 = s32[8,16,128]{2,1,0:T(8,128)S(1)} copy-done((s32[8,16,128]{2,1,0:T(8,128)S(1)}, s32[8,16,128]{2,1,0:T(8,128)}, u32[]{:S(2)}) %copy-start.2) | copy-done | bytes 65560
  5.1 62.3 %shard_map.86 = (f32[2048,128]{1,0:T(8,128)S(1)}, f32[1,128]{1,0:T(1,128)S(1)}) custom-call(f32[4]{0:T(128)S(1)} %multiply_add_fusion.therm, f32[2048,128]{1,0:T(8,128)S(1)} %bitcast.9, bf16[2048,128]{1,0:T(8,128)(2,1)S(1)} %bitcast.11, s32[128,128]{1,0:T(8,128)S(1)} %bitcast.12, s32[16,128]{1,0:T(8,128)S(1)} %copy-done.3, f32[2,128]{1,0:T(2,128)S(1)} %bitcast.13, ...), custom_call_target="tpu_custom_call" | custom-call | tf_op jit(solution)/shard_map/pallas_call | solution.py:421
  67.5 0.5 slice_bitcast_fusion
  68.0 1.0 %copy.11 = f32[8,16,16,128]{3,2,1,0:T(8,128)} copy(f32[8,16,16,128]{3,2,1,0:T(8,128)S(1)} %bitcast.10) | data formatting | bytes 2097152
  (1 shorter events, 0.0 us)
Async XLA Ops:
  1.3 0.7 %copy-start.3 = (s32[16,128]{1,0:T(8,128)S(1)}, s32[16,128]{1,0:T(8,128)}, u32[]{:S(2)}) copy-start(s32[16,128]{1,0:T(8,128)} %counts.1) | copy-start | bytes 24580
  1.3 0.7 copy-start.5
  1.3 0.7 copy-start.4
  2.0 1.2 %copy-start = (f32[8,16,16,128]{3,2,1,0:T(8,128)S(1)}, f32[8,16,16,128]{3,2,1,0:T(8,128)}, u32[]{:S(2)}) copy-start(f32[8,16,16,128]{3,2,1,0:T(8,128)} %param.7) | copy-start | bytes 3145732
  3.3 1.0 %copy-start.1 = (bf16[8,16,16,128]{3,2,1,0:T(8,128)(2,1)S(1)}, bf16[8,16,16,128]{3,2,1,0:T(8,128)(2,1)}, u32[]{:S(2)}) copy-start(bf16[8,16,16,128]{3,2,1,0:T(8,128)(2,1)} %param.8) | copy-start | bytes 1572868
  4.3 0.8 %copy-start.2 = (s32[8,16,128]{2,1,0:T(8,128)S(1)}, s32[8,16,128]{2,1,0:T(8,128)}, u32[]{:S(2)}) copy-start(s32[8,16,128]{2,1,0:T(8,128)} %param.9) | copy-start | bytes 196612

commit v2 on v1

--- a/solution.py
+++ b/solution.py
@@ -33,7 +33,7 @@
     out, gout,
     p0, p1, p2, p3, a4, a3, a2, a1, drive0, seed32,
     live, index, match, moba, act, pos, gacc, ones,
-    xh, ye, yh, hc, le, lxh, lyh,
+    xh, ye, yh, hc, rim_rows, le, lxh, lyh,
     gs, g3, r1, s2, r2,
     xs_sem, xr_sem, ys_sem, yr_sem, ls_sem, lr_sem, s1_sem, q1_sem, s2_sem, q2_sem,
 ):
@@ -92,9 +92,23 @@
         packed = jnp.zeros((slots, LANES), jnp.float32)
         for z, value in enumerate(values):
             packed = jnp.where(pair == z, pltpu.roll(value, 2 * z + 1, 1), packed)
-        part = lax.rem(x, per)
-        packed = pltpu.roll(packed, part * (2 * depth), 1)
-        ye[e, x // per] = jnp.where(group == part, packed, ye[e, x // per])
+        rim_rows[e, x] = packed
+
+    def fill_sides(e):
+        for i in range(packs):
+            whole = rim_rows[e, i * per]
+            for part in range(1, per):
+                turned = pltpu.roll(rim_rows[e, i * per + part], part * (2 * depth), 1)
+                whole = jnp.where(group == part, turned, whole)
+            ye[e, i] = whole
+
+    def rows_in(start, stop, by, body):
+        def several(i, carry):
+            for q in range(by):
+                body(start + i * by + q)
+            return carry
+
+        lax.fori_loop(0, (stop - start) // by, several, 0)
 
     mob_tables = [jnp.broadcast_to(mob[r : r + 1, :], (slots, LANES)) for r in range(mob.shape[0])]
     pos_tables = [jnp.broadcast_to(opos[r : r + 1, :], (slots, LANES)) for r in range(opos.shape[0])]
@@ -111,7 +125,6 @@
         pos[x] = lookup(pos_tables, own)
         gacc[x] = jnp.zeros((slots, LANES), jnp.float32)
     le[...] = edge
-    ye[...] = jnp.zeros(ye.shape, jnp.float32)
     span = slots * depth
     ones[...] = jnp.where(
         lax.broadcasted_iota(jnp.int32, (span, span), 0) // slots
@@ -119,7 +132,7 @@
         0.25, 0.0,
     ).astype(jnp.bfloat16)
 
-    def load_phase(x, carry):
+    def load_phase(x):
         active = act[x]
         values = []
         for z in range(depth):
@@ -127,9 +140,8 @@
             p0[x, z] = value
             values.append(value)
         pack_row(0, x, values)
-        return carry
-
-    lax.fori_loop(0, rows, load_phase, 0)
+
+    rows_in(0, rows, 4, load_phase)
 
     pl.semaphore_wait(barrier, (nx - 1) + (ny - 1))
     id_copies = (
@@ -149,6 +161,7 @@
     sent = list(id_copies)
 
     def launch(e, src):
+        fill_sides(e)
         xc, yc = x_copies(e, src), y_copies(e)
         for c in yc + xc:
             c.start()
@@ -166,7 +179,7 @@
 
     lax.fori_loop(0, seed.shape[0] // 128, widen, 0)
 
-    def load_seed(x, carry):
+    def load_seed(x):
         active = act[x]
         values = []
         for z in range(depth):
@@ -174,9 +187,8 @@
             a4[x, z] = value
             values.append(value)
         pack_row(3, x, values)
-        return carry
-
-    lax.fori_loop(0, rows, load_seed, 0)
+
+    rows_in(0, rows, 4, load_seed)
     flight[3] = launch(3, a4)
 
     for c in id_copies:
@@ -185,7 +197,7 @@
     live[rows + 1] = lxh[1]
     id_sides = swap_sides(lyh[0], lyh[1])
 
-    def match_row(x, carry):
+    def match_row(x):
         own = live[x + 1]
         side = pltpu.roll(id_sides, LANES - 1 - 2 * x, 1)
         beside = (
@@ -203,25 +215,25 @@
                 hit = jnp.where(same, 1.0, hit)
             index[n, x] = where
             match[n, x] = hit
-        return carry
-
-    lax.fori_loop(0, rows, match_row, 0)
+
+    rows_in(0, rows, 4, match_row)
 
     def open_sides(e):
         for c in flight[e][1]:
             c.wait_recv()
         for i in range(packs):
-            hc[e, i] = swap_sides(yh[e, 0, i], yh[e, 1, i])
+            sides = swap_sides(yh[e, 0, i], yh[e, 1, i])
+            for part in range(per):
+                hc[e, i * per + part] = pltpu.roll(sides, LANES - 1 - part * (2 * depth), 1)
 
     def lateral(e, x, centre, up, down):
-        part = lax.rem(x, per)
-        side_row = pltpu.roll(hc[e, x // per], lax.rem(LANES - part * (2 * depth), LANES), 1)
+        side_row = hc[e, x]
         where = [index[n, x] for n in range(4)]
         hit = [match[n, x] for n in range(4)]
         totals = []
         for z in range(depth):
             c = centre[z]
-            side = pltpu.roll(side_row, LANES - 1 - 2 * z, 1)
+            side = side_row if z == 0 else pltpu.roll(side_row, LANES - 2 * z, 1)
             left = jnp.where(first, side, pltpu.roll(c, 1, 1))
             right = jnp.where(final, side, pltpu.roll(c, LANES - 1, 1))
             total = (
@@ -291,36 +303,17 @@
             pack_row(e + 1, x, values)
 
     def inner(row, s, src):
-        def body(x, carry):
+        def body(x):
             row(s, x, lambda z: src[x - 1, z], lambda z: src[x + 1, z])
-            return carry
-
-        lax.fori_loop(1, rows - 1, body, 0)
+
+        rows_in(1, rows - 1, 2, body)
 
     def rim(row, s, src, e):
         for c in flight[e][0]:
             c.wait_recv()
 
-        def top(z):
-            return xh[e, 0, z]
-
-        def bottom(z):
-            return xh[e, 1, z]
-
-        def body(i, carry):
-            x = i * (rows - 1)
-            low = i == 0
-
-            def up(z):
-                return jnp.where(low, xh[e, 0, z], src[rows - 2, z])
-
-            def down(z):
-                return jnp.where(low, src[1, z], xh[e, 1, z])
-
-            row(s, x, up, down)
-            return carry
-
-        lax.fori_loop(0, 2, body, 0)
+        row(s, 0, lambda z: xh[e, 0, z], lambda z: src[1, z])
+        row(s, rows - 1, lambda z: src[rows - 2, z], lambda z: xh[e, 1, z])
 
     for s in range(STEPS - 1):
         open_sides(s)
@@ -338,7 +331,7 @@
 
     which = lax.broadcasted_iota(jnp.int32, (ndev, LANES), 0)
 
-    def gather_grains(x, total):
+    def gather_grains(x):
         value = 0.05 * gacc[x]
         spot = pos[x]
         owner = spot // out_per
@@ -353,10 +346,15 @@
             terms.append(jnp.concatenate([coarse, term - coarse], axis=0))
         pick = jnp.concatenate(picks, axis=1).astype(jnp.bfloat16)
         term = jnp.concatenate(terms, axis=1).astype(jnp.bfloat16)
-        return total + lax.dot_general(
+        return lax.dot_general(
             pick, term, (((1,), (1,)), ((), ())), preferred_element_type=jnp.float32)
 
-    total = lax.fori_loop(0, rows, gather_grains, jnp.zeros((ndev, 2 * slots), jnp.float32))
+    def gather_rows(i, total):
+        for q in range(4):
+            total = total + gather_grains(4 * i + q)
+        return total
+
+    total = lax.fori_loop(0, rows // 4, gather_rows, jnp.zeros((ndev, 2 * slots), jnp.float32))
     gs[...] = jnp.zeros(gs.shape, jnp.float32)
     gs[:, 0 : 2 * slots] = total
     for d in range(ndev):
@@ -438,7 +436,8 @@
             pltpu.VMEM((EXCHANGES, 2, depth, slots, cols), jnp.float32),
             pltpu.VMEM((EXCHANGES, packs, slots, LANES), jnp.float32),
             pltpu.VMEM((EXCHANGES, 2, packs, slots, LANES), jnp.float32),
-            pltpu.VMEM((EXCHANGES, packs, slots, LANES), jnp.float32),
+            pltpu.VMEM((EXCHANGES, rows, slots, LANES), jnp.float32),
+            pltpu.VMEM((EXCHANGES, rows, slots, LANES), jnp.float32),
             pltpu.VMEM((slots, LANES), jnp.int32),
             pltpu.VMEM((2, slots, LANES), jnp.int32),
             pltpu.VMEM((2, slots, LANES), jnp.int32),

time: 69.3 us -> 52.3 us (0.75)
  Pallas kernels: 62.3 us -> 45.3 us
    pallas_call x1, Pallas kernels: 62.3 us -> 45.3 us  [shards(): pl.pallas_call(functools.partial(kernel, nx, ny, slots, depth, rows, out_...]
where the time goes in v2:
time: 52.3 us; the launch traced here: 52 us
  Pallas kernels  45.3 us (87%)
  local copies, waits for them, and re-layouts  5.27 us (10%)
  between operations  1.31 us (3%)
    pallas_call x1, Pallas kernels, shards(): pl.pallas_call(functools.partial(kernel, nx, ny, slots, depth, rows, out_...  45.3 us
    unnamed x13, local copies, waits for them, and re-layouts  4.76 us

profile of v2, /device:TPU:0, one launch (start us, length us, event | category | flops | bytes accessed | tf_op | source)
XLA Modules:
  0.0 52.0 jit_solution(4486500784130391008)
XLA Ops:
  1.3 0.0 copy-start.3
  1.3 0.0 copy-start.5
  1.3 0.0 copy-start.4
  1.4 0.6 %copy-done.3 = s32[16,128]{1,0:T(8,128)S(1)} copy-done((s32[16,128]{1,0:T(8,128)S(1)}, s32[16,128]{1,0:T(8,128)}, u32[]{:S(2)}) %copy-start.3) | copy-done | bytes 8216
  2.0 0.0 copy-done.5
  2.0 0.0 copy-done.4
  2.0 0.0 copy-start
  2.0 1.2 %copy-done = f32[8,16,16,128]{3,2,1,0:T(8,128)S(1)} copy-done((f32[8,16,16,128]{3,2,1,0:T(8,128)S(1)}, f32[8,16,16,128]{3,2,1,0:T(8,128)}, u32[]{:S(2)}) %copy-start) | copy-done | bytes 1048600
  3.3 0.0 copy-start.1
  3.3 1.0 %copy-done.1 = bf16[8,16,16,128]{3,2,1,0:T(8,128)(2,1)S(1)} copy-done((bf16[8,16,16,128]{3,2,1,0:T(8,128)(2,1)S(1)}, bf16[8,16,16,128]{3,2,1,0:T(8,128)(2,1)}, u32[]{:S(2)}) %copy-start.1) | copy-done | bytes 524312
  4.3 0.0 copy-start.2
  4.3 0.8 %copy-done.2 = s32[8,16,128]{2,1,0:T(8,128)S(1)} copy-done((s32[8,16,128]{2,1,0:T(8,128)S(1)}, s32[8,16,128]{2,1,0:T(8,128)}, u32[]{:S(2)}) %copy-start.2) | copy-done | bytes 65560
  5.1 45.3 %shard_map.86 = (f32[2048,128]{1,0:T(8,128)S(1)}, f32[1,128]{1,0:T(1,128)S(1)}) custom-call(f32[4]{0:T(128)S(1)} %multiply_add_fusion.therm, f32[2048,128]{1,0:T(8,128)S(1)} %bitcast.9, bf16[2048,128]{1,0:T(8,128)(2,1)S(1)} %bitcast.11, s32[128,128]{1,0:T(8,128)S(1)} %bitcast.12, s32[16,128]{1,0:T(8,128)S(1)} %copy-done.3, f32[2,128]{1,0:T(2,128)S(1)} %bitcast.13, ...), custom_call_target="tpu_custom_call" | custom-call | tf_op jit(solution)/shard_map/pallas_call | solution.py:419
  50.5 0.5 slice_bitcast_fusion
  51.0 1.0 %copy.11 = f32[8,16,16,128]{3,2,1,0:T(8,128)} copy(f32[8,16,16,128]{3,2,1,0:T(8,128)S(1)} %bitcast.10) | data formatting | bytes 2097152
  (1 shorter events, 0.0 us)
Async XLA Ops:
  1.3 0.7 %copy-start.3 = (s32[16,128]{1,0:T(8,128)S(1)}, s32[16,128]{1,0:T(8,128)}, u32[]{:S(2)}) copy-start(s32[16,128]{1,0:T(8,128)} %counts.1) | copy-start | bytes 24580
  1.3 0.7 %copy-start.5 = (s32[256]{0:T(256)S(1)}, s32[256]{0:T(256)}, u32[]{:S(2)}) copy-start(s32[256]{0:T(256)} %param.12) | copy-start | bytes 3076
  1.3 0.7 %copy-start.4 = (f32[256]{0:T(256)S(1)}, f32[256]{0:T(256)}, u32[]{:S(2)}) copy-start(f32[256]{0:T(256)} %param.11) | copy-start | bytes 3076
  2.0 1.2 %copy-start = (f32[8,16,16,128]{3,2,1,0:T(8,128)S(1)}, f32[8,16,16,128]{3,2,1,0:T(8,128)}, u32[]{:S(2)}) copy-start(f32[8,16,16,128]{3,2,1,0:T(8,128)} %param.7) | copy-start | bytes 3145732
  3.3 1.0 %copy-start.1 = (bf16[8,16,16,128]{3,2,1,0:T(8,128)(2,1)S(1)}, bf16[8,16,16,128]{3,2,1,0:T(8,128)(2,1)}, u32[]{:S(2)}) copy-start(bf16[8,16,16,128]{3,2,1,0:T(8,128)(2,1)} %param.8) | copy-start | bytes 1572868
  4.3 0.8 %copy-start.2 = (s32[8,16,128]{2,1,0:T(8,128)S(1)}, s32[8,16,128]{2,1,0:T(8,128)}, u32[]{:S(2)}) copy-start(s32[8,16,128]{2,1,0:T(8,128)} %param.9) | copy-start | bytes 196612

commit v3 on v2

--- a/solution.py
+++ b/solution.py
@@ -41,7 +41,9 @@
     gy = lax.axis_index("gy")
     ndev = nx * ny
     per = LANES // (2 * depth)
-    packs = rows // per
+    pieces = ((0, 2), (2, 4), (4, 5))
+    cut = 1 + 2 * per
+    used = [x for x in range(rows - 2)] + [4 * per, 4 * per + 1]
     stride = depth * rows
     phases = (p0, p1, p2, p3)
     adjoints = {4: a4, 3: a3, 2: a2, 1: a1}
@@ -75,29 +77,30 @@
                 recv_sem=xr_sem.at[e, 1], device_id=low_x, device_id_type=MESH),
         )
 
-    def y_copies(e):
-        return (
+    def y_copies(e, p):
+        block = pl.ds(pieces[p][0], pieces[p][1] - pieces[p][0])
+        return [
             pltpu.make_async_remote_copy(
-                src_ref=ye.at[e], dst_ref=yh.at[e, 0], send_sem=ys_sem.at[e, 0],
-                recv_sem=yr_sem.at[e, 0], device_id=high_y, device_id_type=MESH),
-            pltpu.make_async_remote_copy(
-                src_ref=ye.at[e], dst_ref=yh.at[e, 1], send_sem=ys_sem.at[e, 1],
-                recv_sem=yr_sem.at[e, 1], device_id=low_y, device_id_type=MESH),
-        )
+                src_ref=ye.at[e, block], dst_ref=yh.at[e, side, block], send_sem=ys_sem.at[e, p, side],
+                recv_sem=yr_sem.at[e, p, side], device_id=target, device_id_type=MESH)
+            for side, target in enumerate((high_y, low_y))
+        ]
 
     def swap_sides(from_low, from_high):
         return jnp.where(even, pltpu.roll(from_high, LANES - 1, 1), pltpu.roll(from_low, 1, 1))
 
-    def pack_row(e, x, values):
+    def pack_row(e, slot, values):
         packed = jnp.zeros((slots, LANES), jnp.float32)
         for z, value in enumerate(values):
             packed = jnp.where(pair == z, pltpu.roll(value, 2 * z + 1, 1), packed)
-        rim_rows[e, x] = packed
-
-    def fill_sides(e):
-        for i in range(packs):
+        rim_rows[e, slot] = packed
+
+    def fill_sides(e, p):
+        for i in range(*pieces[p]):
             whole = rim_rows[e, i * per]
             for part in range(1, per):
+                if i * per + part not in used:
+                    continue
                 turned = pltpu.roll(rim_rows[e, i * per + part], part * (2 * depth), 1)
                 whole = jnp.where(group == part, turned, whole)
             ye[e, i] = whole
@@ -132,16 +135,18 @@
         0.25, 0.0,
     ).astype(jnp.bfloat16)
 
-    def load_phase(x):
+    def load_phase(x, slot):
         active = act[x]
         values = []
         for z in range(depth):
             value = sf[pl.ds(z * rows + x, slots, stride=stride), :] * active
             p0[x, z] = value
             values.append(value)
-        pack_row(0, x, values)
-
-    rows_in(0, rows, 4, load_phase)
+        pack_row(0, slot, values)
+
+    rows_in(1, rows - 1, 2, lambda x: load_phase(x, x - 1))
+    load_phase(0, 4 * per)
+    load_phase(rows - 1, 4 * per + 1)
 
     pl.semaphore_wait(barrier, (nx - 1) + (ny - 1))
     id_copies = (
@@ -160,17 +165,29 @@
     )
     sent = list(id_copies)
 
-    def launch(e, src):
-        fill_sides(e)
-        xc, yc = x_copies(e, src), y_copies(e)
-        for c in yc + xc:
+    flight = {}
+
+    def launch_y(e, p):
+        fill_sides(e, p)
+        flight[e, p] = y_copies(e, p)
+        for c in flight[e, p]:
             c.start()
             sent.append(c)
-        return xc, yc
+
+    def launch_x(e, src):
+        flight[e, "x"] = x_copies(e, src)
+        for c in flight[e, "x"]:
+            c.start()
+            sent.append(c)
+
+    def launch(e, src):
+        for p in range(len(pieces)):
+            launch_y(e, p)
+        launch_x(e, src)
 
     for c in id_copies:
         c.start()
-    flight = {0: launch(0, p0)}
+    launch(0, p0)
 
     def widen(i, carry):
         block = pl.ds(pl.multiple_of(i * 128, 128), 128)
@@ -179,17 +196,19 @@
 
     lax.fori_loop(0, seed.shape[0] // 128, widen, 0)
 
-    def load_seed(x):
+    def load_seed(x, slot):
         active = act[x]
         values = []
         for z in range(depth):
             value = seed32[pl.ds(z * rows + x, slots, stride=stride), :] * active
             a4[x, z] = value
             values.append(value)
-        pack_row(3, x, values)
-
-    rows_in(0, rows, 4, load_seed)
-    flight[3] = launch(3, a4)
+        pack_row(3, slot, values)
+
+    rows_in(1, rows - 1, 2, lambda x: load_seed(x, x - 1))
+    load_seed(0, 4 * per)
+    load_seed(rows - 1, 4 * per + 1)
+    launch(3, a4)
 
     for c in id_copies:
         c.wait_recv()
@@ -218,16 +237,18 @@
 
     rows_in(0, rows, 4, match_row)
 
-    def open_sides(e):
-        for c in flight[e][1]:
+    def open_sides(e, p):
+        for c in flight[e, p]:
             c.wait_recv()
-        for i in range(packs):
+        for i in range(*pieces[p]):
             sides = swap_sides(yh[e, 0, i], yh[e, 1, i])
             for part in range(per):
+                if i * per + part not in used:
+                    continue
                 hc[e, i * per + part] = pltpu.roll(sides, LANES - 1 - part * (2 * depth), 1)
 
-    def lateral(e, x, centre, up, down):
-        side_row = hc[e, x]
+    def lateral(e, x, slot, centre, up, down):
+        side_row = hc[e, slot]
         where = [index[n, x] for n in range(4)]
         hit = [match[n, x] for n in range(4)]
         totals = []
@@ -251,12 +272,12 @@
         sums = jnp.dot(ones[...], stacked, preferred_element_type=jnp.float32)
         return [sums[z * slots : (z + 1) * slots] for z in range(depth)]
 
-    def forward_row(s, x, up, down):
+    def forward_row(s, x, slot, up, down):
         src, dst = phases[s], phases[s + 1]
         centre = [src[x, z] for z in range(depth)]
         rate = therm[s] * moba[x]
         crowd = slot_sums(centre)
-        totals = lateral(s, x, centre, up, down)
+        totals = lateral(s, x, slot, centre, up, down)
         values = []
         for z in range(depth):
             c = centre[z]
@@ -267,9 +288,9 @@
             dst[x, z] = value
             values.append(value)
         if s + 1 < STEPS - 1:
-            pack_row(s + 1, x, values)
-
-    def backward_row(s, x, up, down):
+            pack_row(s + 1, slot, values)
+
+    def backward_row(s, x, slot, up, down):
         src, phase = adjoints[s + 1], phases[s]
         e = 3 + (STEPS - 1 - s)
         active = act[x]
@@ -278,7 +299,7 @@
         c = [phase[x, z] for z in range(depth)]
         crowd = slot_sums(c)
         shared = slot_sums([rate * centre[z] * c[z] for z in range(depth)])
-        totals = lateral(e, x, centre, up, down)
+        totals = lateral(e, x, slot, centre, up, down)
         values = []
         now = jnp.zeros((slots, LANES), jnp.float32)
         before = jnp.zeros((slots, LANES), jnp.float32)
@@ -300,34 +321,42 @@
             if s == 1:
                 gained = gained + therm[0] * before
             gacc[x] = gained
-            pack_row(e + 1, x, values)
-
-    def inner(row, s, src):
+            pack_row(e + 1, slot, values)
+
+    def inner(row, s, src, e, after):
         def body(x):
-            row(s, x, lambda z: src[x - 1, z], lambda z: src[x + 1, z])
-
-        rows_in(1, rows - 1, 2, body)
+            row(s, x, x - 1, lambda z: src[x - 1, z], lambda z: src[x + 1, z])
+
+        open_sides(e, 0)
+        rows_in(1, cut, 2, body)
+        if after is not None:
+            launch_y(after, 0)
+        open_sides(e, 1)
+        rows_in(cut, rows - 1, 2, body)
+        if after is not None:
+            launch_y(after, 1)
 
     def rim(row, s, src, e):
-        for c in flight[e][0]:
+        open_sides(e, 2)
+        for c in flight[e, "x"]:
             c.wait_recv()
-
-        row(s, 0, lambda z: xh[e, 0, z], lambda z: src[1, z])
-        row(s, rows - 1, lambda z: src[rows - 2, z], lambda z: xh[e, 1, z])
+        row(s, 0, 4 * per, lambda z: xh[e, 0, z], lambda z: src[1, z])
+        row(s, rows - 1, 4 * per + 1, lambda z: src[rows - 2, z], lambda z: xh[e, 1, z])
 
     for s in range(STEPS - 1):
-        open_sides(s)
-        inner(forward_row, s, phases[s])
+        after = s + 1 if s + 1 < STEPS - 1 else None
+        inner(forward_row, s, phases[s], s, after)
         rim(forward_row, s, phases[s], s)
-        if s + 1 < STEPS - 1:
-            flight[s + 1] = launch(s + 1, phases[s + 1])
+        if after is not None:
+            launch_x(after, phases[s + 1])
+            launch_y(after, 2)
 
     for s in range(STEPS - 1, 0, -1):
         e = 3 + (STEPS - 1 - s)
-        open_sides(e)
-        inner(backward_row, s, adjoints[s + 1])
+        inner(backward_row, s, adjoints[s + 1], e, e + 1)
         rim(backward_row, s, adjoints[s + 1], e)
-        flight[e + 1] = launch(e + 1, adjoints[s])
+        launch_x(e + 1, adjoints[s])
+        launch_y(e + 1, 2)
 
     which = lax.broadcasted_iota(jnp.int32, (ndev, LANES), 0)
 
@@ -369,8 +398,7 @@
         stage1.append(c)
         sent.append(c)
 
-    open_sides(EXCHANGES - 1)
-    inner(backward_row, 0, a1)
+    inner(backward_row, 0, a1, EXCHANGES - 1, None)
 
     for c in stage1:
         c.wait_recv()
@@ -413,7 +441,9 @@
     flat = slots * depth * rows
     block = pltpu.VMEM((rows, depth, slots, cols), jnp.float32)
     plane = pltpu.VMEM((rows, slots, cols), jnp.float32)
-    packs = rows * 2 * depth // LANES
+    per = LANES // (2 * depth)
+    packs = 5
+    assert rows == 4 * per
     dma = pltpu.SemaphoreType.DMA
     vmem = pl.BlockSpec(memory_space=pltpu.VMEM)
     adjoint, owned = pl.pallas_call(
@@ -436,8 +466,8 @@
             pltpu.VMEM((EXCHANGES, 2, depth, slots, cols), jnp.float32),
             pltpu.VMEM((EXCHANGES, packs, slots, LANES), jnp.float32),
             pltpu.VMEM((EXCHANGES, 2, packs, slots, LANES), jnp.float32),
-            pltpu.VMEM((EXCHANGES, rows, slots, LANES), jnp.float32),
-            pltpu.VMEM((EXCHANGES, rows, slots, LANES), jnp.float32),
+            pltpu.VMEM((EXCHANGES, packs * per, slots, LANES), jnp.float32),
+            pltpu.VMEM((EXCHANGES, packs * per, slots, LANES), jnp.float32),
             pltpu.VMEM((slots, LANES), jnp.int32),
             pltpu.VMEM((2, slots, LANES), jnp.int32),
             pltpu.VMEM((2, slots, LANES), jnp.int32),
@@ -447,7 +477,7 @@
             pltpu.VMEM((ny, 1, LANES), jnp.float32),
             pltpu.VMEM((ny, 1, LANES), jnp.float32),
             dma((EXCHANGES, 2)), dma((EXCHANGES, 2)),
-            dma((EXCHANGES, 2)), dma((EXCHANGES, 2)),
+            dma((EXCHANGES, 3, 2)), dma((EXCHANGES, 3, 2)),
             dma((4,)), dma((4,)),
             dma((nx,)), dma((nx,)), dma((ny,)), dma((ny,)),
         ],

time: 52.3 us -> 52.8 us (level)
  Pallas kernels: 45.3 us -> 45.9 us
    pallas_call x1, Pallas kernels: 45.3 us -> 45.9 us  [shards(): pl.pallas_call(functools.partial(kernel, nx, ny, slots, depth, rows, out_...]
where the time goes in v3:
time: 52.8 us; the launch traced here: 52.5 us
  Pallas kernels  45.9 us (87%)
  local copies, waits for them, and re-layouts  5.27 us (10%)
  between operations  1.31 us (2%)
    pallas_call x1, Pallas kernels, shards(): pl.pallas_call(functools.partial(kernel, nx, ny, slots, depth, rows, out_...  45.9 us
    unnamed x13, local copies, waits for them, and re-layouts  4.76 us

profile of v3, /device:TPU:0, one launch (start us, length us, event | category | flops | bytes accessed | tf_op | source)
XLA Modules:
  0.0 52.5 jit_solution(17905282233319957666)
XLA Ops:
  1.3 0.0 copy-start.3
  1.3 0.0 copy-start.5
  1.3 0.0 copy-start.4
  1.4 0.6 %copy-done.3 = s32[16,128]{1,0:T(8,128)S(1)} copy-done((s32[16,128]{1,0:T(8,128)S(1)}, s32[16,128]{1,0:T(8,128)}, u32[]{:S(2)}) %copy-start.3) | copy-done | bytes 8216
  2.0 0.0 copy-done.5
  2.0 0.0 copy-done.4
  2.0 0.0 copy-start
  2.0 1.2 %copy-done = f32[8,16,16,128]{3,2,1,0:T(8,128)S(1)} copy-done((f32[8,16,16,128]{3,2,1,0:T(8,128)S(1)}, f32[8,16,16,128]{3,2,1,0:T(8,128)}, u32[]{:S(2)}) %copy-start) | copy-done | bytes 1048600
  3.3 0.0 copy-start.1
  3.3 1.0 %copy-done.1 = bf16[8,16,16,128]{3,2,1,0:T(8,128)(2,1)S(1)} copy-done((bf16[8,16,16,128]{3,2,1,0:T(8,128)(2,1)S(1)}, bf16[8,16,16,128]{3,2,1,0:T(8,128)(2,1)}, u32[]{:S(2)}) %copy-start.1) | copy-done | bytes 524312
  4.3 0.0 copy-start.2
  4.3 0.8 %copy-done.2 = s32[8,16,128]{2,1,0:T(8,128)S(1)} copy-done((s32[8,16,128]{2,1,0:T(8,128)S(1)}, s32[8,16,128]{2,1,0:T(8,128)}, u32[]{:S(2)}) %copy-start.2) | copy-done | bytes 65560
  5.1 45.9 %shard_map.86 = (f32[2048,128]{1,0:T(8,128)S(1)}, f32[1,128]{1,0:T(1,128)S(1)}) custom-call(f32[4]{0:T(128)S(1)} %multiply_add_fusion.therm, f32[2048,128]{1,0:T(8,128)S(1)} %bitcast.9, bf16[2048,128]{1,0:T(8,128)(2,1)S(1)} %bitcast.11, s32[128,128]{1,0:T(8,128)S(1)} %bitcast.12, s32[16,128]{1,0:T(8,128)S(1)} %copy-done.3, f32[2,128]{1,0:T(2,128)S(1)} %bitcast.13, ...), custom_call_target="tpu_custom_call" | custom-call | tf_op jit(solution)/shard_map/pallas_call | solution.py:449
  51.0 0.5 slice_bitcast_fusion
  51.5 1.0 %copy.11 = f32[8,16,16,128]{3,2,1,0:T(8,128)} copy(f32[8,16,16,128]{3,2,1,0:T(8,128)S(1)} %bitcast.10) | data formatting | bytes 2097152
  (1 shorter events, 0.0 us)
Async XLA Ops:
  1.3 0.7 %copy-start.3 = (s32[16,128]{1,0:T(8,128)S(1)}, s32[16,128]{1,0:T(8,128)}, u32[]{:S(2)}) copy-start(s32[16,128]{1,0:T(8,128)} %counts.1) | copy-start | bytes 24580
  1.3 0.7 %copy-start.5 = (s32[256]{0:T(256)S(1)}, s32[256]{0:T(256)}, u32[]{:S(2)}) copy-start(s32[256]{0:T(256)} %param.12) | copy-start | bytes 3076
  1.3 0.7 %copy-start.4 = (f32[256]{0:T(256)S(1)}, f32[256]{0:T(256)}, u32[]{:S(2)}) copy-start(f32[256]{0:T(256)} %param.11) | copy-start | bytes 3076
  2.0 1.2 %copy-start = (f32[8,16,16,128]{3,2,1,0:T(8,128)S(1)}, f32[8,16,16,128]{3,2,1,0:T(8,128)}, u32[]{:S(2)}) copy-start(f32[8,16,16,128]{3,2,1,0:T(8,128)} %param.7) | copy-start | bytes 3145732
  3.3 1.0 %copy-start.1 = (bf16[8,16,16,128]{3,2,1,0:T(8,128)(2,1)S(1)}, bf16[8,16,16,128]{3,2,1,0:T(8,128)(2,1)}, u32[]{:S(2)}) copy-start(bf16[8,16,16,128]{3,2,1,0:T(8,128)(2,1)} %param.8) | copy-start | bytes 1572868
  4.3 0.8 %copy-start.2 = (s32[8,16,128]{2,1,0:T(8,128)S(1)}, s32[8,16,128]{2,1,0:T(8,128)}, u32[]{:S(2)}) copy-start(s32[8,16,128]{2,1,0:T(8,128)} %param.9) | copy-start | bytes 196612
